TPU v7x, 32 devices: a whole 2x2x4 slice. The times are simulated.
32 devices in a mesh: expert: 4 (over z), dp: 8 (over y, x, core).
Axes of the slice: x: 2, y: 2, z: 4, core: 2. Of those that a mesh axis runs over, the one named last changes fastest.
Arguments:
- gradient: float32 [4, 8, 512, 1024], P('expert', 'dp'), may hold values from -200 to 200
- first_moment: float32 [4, 512, 1024], P('expert', 'dp'), may hold values from -0.6 to 0.6
- second_moment: float32 [4, 512, 1024], P('expert', 'dp'), may hold values from 0.002 to 0.02
- left_basis: float32 [4, 512, 512], P('expert'), may hold values from -1 to 1
- right_basis: float32 [4, 2, 512, 512], P('expert'), may hold values from -1 to 1
Outputs:
- update: float32 [4, 512, 1024], P('expert')
- new_first: float32 [4, 512, 1024], P('expert', 'dp')
- new_second: float32 [4, 512, 1024], P('expert', 'dp')
All inputs are finite; a program needn't handle non-finite values.
Results may differ from a plain program's by a relative error of at most 0.000092.
Values sent between devices are 32-bit elements; how exact they have to be, the bound alone decides.
A program may use at most 64 MiB of HBM per device.

v0:
```python
import jax
import jax.numpy as jnp
from jax import lax
from jax.sharding import PartitionSpec as P

highest = lax.Precision.HIGHEST


def right_turn(values, basis):
    blocks = basis.shape[1]
    order = basis.shape[2]
    parts = values.reshape(values.shape[0], values.shape[1], blocks, order)
    out = jnp.einsum("erbc,ebcd->erbd", parts, basis, precision=highest)
    return out.reshape(values.shape)


def right_back(values, basis):
    blocks = basis.shape[1]
    order = basis.shape[2]
    parts = values.reshape(values.shape[0], values.shape[1], blocks, order)
    out = jnp.einsum("erbd,ebcd->erbc", parts, basis, precision=highest)
    return out.reshape(values.shape)


def per_device(gradient, first_moment, second_moment, left_basis, right_basis):
    local_grad = gradient[:, 0]
    experts, order, width = local_grad.shape
    replicas = lax.axis_size("dp")
    columns = left_basis
    left = jnp.einsum("ekr,ekc->erc", columns, local_grad, precision=highest)
    summed = lax.psum_scatter(
        jnp.transpose(right_turn(left, right_basis), (1, 0, 2)),
        "dp",
        scatter_dimension=0,
        tiled=True,
    )
    summed = jnp.transpose(summed, (1, 0, 2))
    mean = summed / replicas
    new_first = 0.9 * first_moment + 0.1 * mean
    new_second = 0.95 * second_moment + 0.05 * mean * mean
    normal = new_first / (jnp.sqrt(new_second) + 1e-08)
    total = lax.psum(jnp.sum(normal * normal), ("expert", "dp"))
    count = experts * lax.axis_size("expert") * order * width
    scale = jnp.sqrt(total / count + 1e-06)
    turned = right_back(normal, right_basis)
    columns = left_basis
    back = jnp.einsum(
        "ekr,erc->ekc", columns, lax.all_gather(turned, "dp", axis=1, tiled=True), precision=highest
    )
    return (back / scale, new_first, new_second)


def solution(mesh):
    in_specs = (
        P("expert", "dp", None, None),
        P("expert", "dp", None),
        P("expert", "dp", None),
        P("expert", None, None),
        P("expert", None, None, None),
    )
    out_specs = (P("expert", None, None), P("expert", "dp", None), P("expert", "dp", None))
    return jax.shard_map(
        per_device, mesh=mesh, in_specs=in_specs, out_specs=out_specs, check_vma=False
    )
```

profile of v0, /device:TPU:1, one launch (start us, length us, event | category | flops | bytes accessed | tf_op | source)
XLA Modules:
  0.0 129.7 jit_solution(1113376364364047607)
XLA Ops:
  7.2 0.0 copy-start
  7.2 0.0 reduce-scatter.2.cloned.1.call-start
  7.2 5.5 %fusion = f32[512,2,512]{2,0,1:T(8,128)S(1)} fusion(f32[64,2,8,512]{3,2,1,0:T(8,128)} %bitcast.52, f32[1,512,512]{2,1,0:T(8,128)} %param.8), kind=kOutput, calls=%fused_computation | convolution fusion | flops 3221225472 | bytes 5242880 | tf_op jit(solution)/shard_map/ekr,ekc->erc/dot_general | solution.py:30
  12.8 0.0 copy-done
  12.8 4.9 %fusion.7 = f32[2,512,512]{1,2,0:T(8,128)} fusion(f32[512,2,512]{2,0,1:T(8,128)S(1)} %fusion, f32[1,2,512,512]{3,2,1,0:T(8,128)S(1)} %copy-done), kind=kOutput, calls=%fused_computation.7 | convolution fusion | flops 3221225472 | bytes 6291456 | tf_op jit(solution)/shard_map/erbc,ebcd->erbd/dot_general | solution.py:13
  17.6 2.9 %copy.13 = f32[512,1,1024]{2,0,1:T(8,128)} copy(f32[512,1,1024]{0,2,1:T(8,128)} %bitcast.51) | data formatting | bytes 4194304 | tf_op jit(solution)/shard_map/transpose;reshape | solution.py:32
  20.6 0.0 copy-start.2
  20.6 0.0 copy-start.3
  20.6 0.0 reduce-scatter.2.cloned.1.call-update
  20.6 0.0 all-gather.2.cloned.1.call-start
  20.7 43.4 %reduce-scatter.2.cloned.1.call-done = f32[64,1,1024]{2,0,1:T(8,128)} async-done(((f32[512,1,1024]{2,0,1:T(8,128)}), f32[64,1,1024]{2,0,1:T(8,128)}) %reduce-scatter.2.cloned.1.call-update) | async-done | bytes 262160 | tf_op jit(solution)/shard_map/reduce_scatter | solution.py:31
  64.0 0.0 copy-done.2
  64.0 0.0 copy-done.3
  64.0 2.5 %multiply_reduce_fusion = (f32[]{:T(128)}, f32[1,64,1024]{2,1,0:T(8,128)}, f32[1,64,1024]{2,1,0:T(8,128)}, f32[1,64,1024]{2,1,0:T(8,128)}) fusion(f32[64,1,1024]{2,0,1:T(8,128)} %reduce-scatter.2.cloned.1.call-done, f32[1,64,1024]{2,1,0:T(8,128)S(1)} %copy-done.2, f32[1,64,1024]{2,1,0:T(8,128)S(1)} %copy-done.3), kind=kLoop, calls=%fused_computation.16 | loop fusion | flops 786431 | bytes 1572868 | tf_op jit(solution)/shard_map/reduce_sum | solution.py:42
  66.5 0.0 copy-start.1
  66.5 1.3 reshape.93
  67.8 2.1 %fusion.11 = f32[1,2,8,8,512]{4,3,2,1,0:T(8,128)S(1)} fusion(f32[1,2,512,512]{3,2,1,0:T(8,128)S(1)} %copy-done, f32[64,2,512]{2,1,0:T(2,128)S(1)} %reshape.93), kind=kOutput, calls=%fused_computation.10 | convolution fusion | flops 402653184 | bytes 2621440 | tf_op jit(solution)/shard_map/erbd,ebcd->erbc/dot_general | solution.py:21
  69.9 0.7 copy.20
  70.7 0.0 all-gather.2.cloned.1.call-update
  70.7 39.1 %psum.7 = f32[]{:T(128)} all-reduce(f32[]{:T(128)} %get-tuple-element.9), channel_id=1, replica_groups=mesh['expert'=4,'dp'=8] {'expert','dp'}, use_global_device_ids=true, to_apply=%region_2.0 | all-reduce | flops 1 | bytes 8 | tf_op jit(solution)/shard_map/psum | solution.py:42
  110.4 0.0 all-gather.2.cloned.1.call-done
  110.4 0.0 copy-done.1
  110.4 9.6 %divide_bitcast_fusion = f32[1,512,1024]{1,2,0:T(8,128)} fusion(f32[1,512,1024]{2,1,0:T(8,128)} %all-gather.2.cloned.1.call-done, f32[1,512,512]{2,1,0:T(8,128)S(1)} %copy-done.1, f32[]{:T(128)S(6)} %sqrt.7), kind=kOutput, calls=%fused_computation.9 | convolution fusion | flops 3221749760 | bytes 5242884 | tf_op jit(solution)/shard_map/ekr,erc->ekc/dot_general | solution.py:47
  120.0 2.9 %copy.16 = f32[1,512,1024]{2,1,0:T(8,128)} copy(f32[1,512,1024]{1,2,0:T(8,128)} %divide_bitcast_fusion) | data formatting | bytes 4194304
Async XLA Ops:
  7.2 5.6 %copy-start = (f32[1,2,512,512]{3,2,1,0:T(8,128)S(1)}, f32[1,2,512,512]{3,2,1,0:T(8,128)}, u32[]{:S(2)}) copy-start(f32[1,2,512,512]{3,2,1,0:T(8,128)} %param.9) | copy-start | bytes 6291460
  7.2 56.9 %reduce-scatter.2.cloned.1.call-start = ((), (), s32[]{:S(2)}) async-start(), calls=%async_computation.1 | async-start | bytes 2359296 | tf_op jit(solution)/shard_map/reduce_scatter | solution.py:31
  20.6 43.5 %copy-start.2 = (f32[1,64,1024]{2,1,0:T(8,128)S(1)}, f32[1,64,1024]{2,1,0:T(8,128)}, u32[]{:S(2)}) copy-start(f32[1,64,1024]{2,1,0:T(8,128)} %param.7) | copy-start | bytes 786436
  20.6 43.5 %copy-start.3 = (f32[1,64,1024]{2,1,0:T(8,128)S(1)}, f32[1,64,1024]{2,1,0:T(8,128)}, u32[]{:S(2)}) copy-start(f32[1,64,1024]{2,1,0:T(8,128)} %param.6) | copy-start | bytes 786436
  20.6 89.8 %all-gather.2.cloned.1.call-start = ((), (), s32[]{:S(2)}) async-start(), calls=%async_computation.2 | async-start | bytes 2359296 | tf_op jit(solution)/shard_map/all_gather | solution.py:48
  66.5 43.9 %copy-start.1 = (f32[1,512,512]{2,1,0:T(8,128)S(1)}, f32[1,512,512]{2,1,0:T(8,128)}, u32[]{:S(2)}) copy-start(f32[1,512,512]{2,1,0:T(8,128)} %param.8) | copy-start | bytes 3145732
Sparse Core Ops, SparseCore 0:
  20.7 43.2 reduce-scatter.1
  70.8 28.4 all-gather.1
where the time goes:
time: 131 us; the launch traced here: 130 us
  waiting for transfers between devices  43.4 us (33%)
  blocking collectives  39.1 us (30%)
  matrix products  22.1 us (17%)
  between operations  14.7 us (11%)
  local copies, waits for them, and re-layouts  7.81 us (6%)
  other arithmetic  2.5 us (2%)
    reduce_scatter x1, waiting for transfers between devices, per_device(): lax.psum_scatter(jnp.transpose(right_turn(left, right_basis), (1, 0, 2)),...  43.4 us
    psum x1, blocking collectives, per_device(): total = lax.psum(jnp.sum(normal * normal), ('expert', 'dp'))  39.1 us
    dot_general x1, matrix products, per_device(): jnp.einsum('ekr,erc->ekc', columns, lax.all_gather(turned, 'dp', axis=1,...  9.57 us
    dot_general x1, matrix products, per_device(): left = jnp.einsum('ekr,ekc->erc', columns, local_grad, precision=highest)  5.54 us
    dot_general x1, matrix products, right_turn(): out = jnp.einsum('erbc,ebcd->erbd', parts, basis, precision=highest)  4.87 us
    another operation x1, local copies, waits for them, and re-layouts, per_device(): jnp.transpose(right_turn(left, right_basis), (1, 0, 2))  2.93 us
    unnamed x9, local copies, waits for them, and re-layouts  2.9 us
  transfers between devices with their start and end apart: 2, of which 1 were waited for; matrix products, arithmetic and copies ran while one was open for 0% of the time, Pallas kernels for 0%

commit v1 on v0

v1 whole, which is shorter than its diff:
```python
import functools

import jax
import jax.numpy as jnp
from jax import lax
from jax.experimental import pallas as pl
from jax.experimental.pallas import tpu as pltpu
from jax.sharding import PartitionSpec as P

MESH = pl.DeviceIdType.MESH
NN = (((1,), (0,)), ((), ()))
NT = (((1,), (1,)), ((), ()))


def split(x):
    hi = x.astype(jnp.bfloat16)
    lo = (x - hi.astype(jnp.float32)).astype(jnp.bfloat16)
    return hi, lo


def dot3(a, b, dims=NN):
    dot = functools.partial(
        lax.dot_general, dimension_numbers=dims, preferred_element_type=jnp.float32
    )
    return dot(a[0], b[0]) + (dot(a[0], b[1]) + dot(a[1], b[0]))


def kernel(
    cfg, grad, first, second, left, right,
    back_out, scale_out, first_out, second_out,
    g, lf, rt, fm, sm, lt, gh, gl, lh, ll, ah, al, rh, rl,
    s1, r1, s2, r2, t, acc, zs, ds, sc,
    in_sem, g_sem, out_sem, b_sem, s1_s, s1_r, s2_s, s2_r, ag_s, ag_r, fw_s, fw_r, z_s, z_r, d_s, d_r,
):
    experts, n, chunk, count = cfg
    order, width = grad.shape
    blocks, depth = right.shape[0], right.shape[1]
    chips, rows = n // 2, order // n
    chunks, per = width // chunk, depth // chunk
    e, d = lax.axis_index("expert"), lax.axis_index("dp")
    chip, core = d // 2, d % 2
    sibling = chip * 2 + (1 - core)

    def other(k):
        return lax.rem(chip + k, chips) * 2 + core

    def source(k):
        return lax.rem(chip + chips - k, chips) * 2 + core

    def remote(src, dst, send, recv, to):
        return pltpu.make_async_remote_copy(
            src_ref=src, dst_ref=dst, send_sem=send, recv_sem=recv, device_id=to, device_id_type=MESH
        )

    barrier = pltpu.get_barrier_semaphore()
    for k in range(1, n):
        pl.semaphore_signal(barrier, inc=1, device_id=(e, lax.rem(d + k, n)), device_id_type=MESH)
    for k in range(1, experts):
        pl.semaphore_signal(barrier, inc=1, device_id=(lax.rem(e + k, experts), d), device_id_type=MESH)

    loads = [
        pltpu.make_async_copy(a, b, in_sem.at[i])
        for i, (a, b) in enumerate(((left, lf), (right, rt), (first, fm), (second, sm)))
    ]
    grads = [
        pltpu.make_async_copy(
            grad.at[:, pl.ds(q * chunk, chunk)], g.at[:, pl.ds(q * chunk, chunk)], g_sem.at[q]
        )
        for q in range(chunks)
    ]
    loads[0].start()
    for c in grads:
        c.start()
    for c in loads[1:]:
        c.start()

    loads[0].wait()
    lt[...] = jnp.transpose(lf[...]).reshape(n, rows, order)
    for side, parity in ((0, 1 - core), (1, core)):
        picked = jnp.concatenate([lt[2 * c + parity] for c in range(chips)], axis=0)
        ah[side], al[side] = split(picked)

    pl.semaphore_wait(barrier, n - 1 + experts - 1)

    sends = []
    firsts = []
    for q in range(chunks):
        cols = pl.ds(q * chunk, chunk)
        grads[q].wait()
        hi, lo = split(g[:, cols])
        gh[:, cols], gl[:, cols] = hi, lo
        s1[q] = dot3((ah[0], al[0]), (hi, lo))
        c = remote(s1.at[q], r1.at[q], s1_s.at[q], s1_r.at[q], (e, sibling))
        c.start()
        firsts.append(c)
    seconds = {}
    for q in range(chunks):
        cols = pl.ds(q * chunk, chunk)
        own = dot3((ah[1], al[1]), (gh[:, cols], gl[:, cols]))
        firsts[q].wait_recv()
        total = own + r1[q]
        for c in range(chips):
            s2[c, q] = total[c * rows : (c + 1) * rows]
        for k in range(1, chips):
            c = remote(
                s2.at[lax.rem(chip + k, chips), q], r2.at[k, q], s2_s.at[k, q], s2_r.at[k, q], (e, other(k))
            )
            c.start()
            seconds[k, q] = c
            sends.append(c)
    lh[...], ll[...] = split(lf[...])
    for c in loads[1:]:
        c.wait()
    for b in range(blocks):
        rh[b], rl[b] = split(rt[b])

    gathers = {}
    forwards = {}
    squares = jnp.zeros((1, 1), jnp.float32)
    for b in range(blocks):
        parts = []
        for q in range(b * per, (b + 1) * per):
            x = s2[chip, q]
            for k in range(1, chips):
                seconds[k, q].wait_recv()
                x = x + r2[k, q]
            parts.append(x)
        x = jnp.concatenate(parts, axis=1)
        cols = pl.ds(b * depth, depth)
        turn = (rh[b], rl[b])
        mean = dot3(split(x), turn) / n
        new_first = 0.9 * fm[:, cols] + 0.1 * mean
        new_second = 0.95 * sm[:, cols] + 0.05 * mean * mean
        normal = new_first / (jnp.sqrt(new_second) + 1e-08)
        t[b, d] = dot3(split(normal), turn, NT)
        for k in range(1, chips):
            c = remote(t.at[b, d], t.at[b, d], ag_s.at[b, k], ag_r.at[b, k], (e, other(k)))
            c.start()
            gathers[b, k] = c
            sends.append(c)
        c = remote(t.at[b, d], t.at[b, d], fw_s.at[b, 0], fw_r.at[b, 0], (e, sibling))
        c.start()
        forwards[b, 0] = c
        fm[:, cols] = new_first
        sm[:, cols] = new_second
        squares = squares + jnp.sum(
            jnp.sum(normal * normal, axis=0, keepdims=True), axis=1, keepdims=True
        )

    outs = [
        pltpu.make_async_copy(fm, first_out, out_sem.at[0]),
        pltpu.make_async_copy(sm, second_out, out_sem.at[1]),
    ]
    for c in outs:
        c.start()
    zs[e] = jnp.broadcast_to(squares, zs.shape[1:])
    tops = []
    for k in range(1, experts):
        c = remote(zs.at[e], zs.at[e], z_s.at[k], z_r.at[k], (lax.rem(e + k, experts), d))
        c.start()
        tops.append(c)

    for b in range(blocks):
        for k in range(1, chips):
            gathers[b, k].wait_recv()
            piece = t.at[b, source(k)]
            c = remote(piece, piece, fw_s.at[b, k], fw_r.at[b, k], (e, sibling))
            c.start()
            forwards[b, k] = c
        if b == 0:
            for c in tops:
                c.wait_recv()
            ds[d] = jnp.sum(zs[...], axis=0)
            peers = []
            for k in range(1, n):
                c = remote(ds.at[d], ds.at[d], d_s.at[k], d_r.at[k], (e, lax.rem(d + k, n)))
                c.start()
                peers.append(c)
        for k in range(chips):
            forwards[b, k].wait_recv()
        for j in range(per):
            cols = pl.ds(b * depth + j * chunk, chunk)
            piece = t[b, :, :, j * chunk : (j + 1) * chunk].reshape(order, chunk)
            acc[:, cols] = dot3((lh[...], ll[...]), split(piece))
        cols = pl.ds(b * depth, depth)
        c = pltpu.make_async_copy(acc.at[:, cols], back_out.at[:, cols], b_sem.at[b])
        c.start()
        outs.append(c)

    for c in peers:
        c.wait_recv()
    sc[...] = jnp.sqrt(jnp.sum(ds[...], axis=0) / count + 1e-06)
    c = pltpu.make_async_copy(sc, scale_out, out_sem.at[2])
    c.start()
    outs.append(c)
    for c in firsts + sends + list(forwards.values()) + tops + peers:
        c.wait_send()
    for c in outs:
        c.wait()


def per_device(gradient, first_moment, second_moment, left_basis, right_basis):
    held, _, order, width = gradient.shape
    blocks, depth = right_basis.shape[1], right_basis.shape[2]
    experts, n = lax.axis_size("expert"), lax.axis_size("dp")
    rows, chips = order // n, n // 2
    chunk = min(256, depth)
    chunks = width // chunk
    half = order // 2
    f32, bf16 = jnp.float32, jnp.bfloat16
    dma = pltpu.SemaphoreType.DMA
    tile = (8, 128)
    scratch = [
        pltpu.VMEM((order, width), f32),
        pltpu.VMEM((order, order), f32),
        pltpu.VMEM((blocks, depth, depth), f32),
        pltpu.VMEM((rows, width), f32),
        pltpu.VMEM((rows, width), f32),
        pltpu.VMEM((n, rows, order), f32),
        pltpu.VMEM((order, width), bf16),
        pltpu.VMEM((order, width), bf16),
        pltpu.VMEM((order, order), bf16),
        pltpu.VMEM((order, order), bf16),
        pltpu.VMEM((2, half, order), bf16),
        pltpu.VMEM((2, half, order), bf16),
        pltpu.VMEM((blocks, depth, depth), bf16),
        pltpu.VMEM((blocks, depth, depth), bf16),
        pltpu.VMEM((chunks, half, chunk), f32),
        pltpu.VMEM((chunks, half, chunk), f32),
        pltpu.VMEM((chips, chunks, rows, chunk), f32),
        pltpu.VMEM((chips, chunks, rows, chunk), f32),
        pltpu.VMEM((blocks, n, rows, depth), f32),
        pltpu.VMEM((order, width), f32),
        pltpu.VMEM((experts,) + tile, f32),
        pltpu.VMEM((n,) + tile, f32),
        pltpu.VMEM(tile, f32),
        dma((4,)), dma((chunks,)), dma((3,)), dma((blocks,)),
        dma((chunks,)), dma((chunks,)),
        dma((chips, chunks)), dma((chips, chunks)),
        dma((blocks, chips)), dma((blocks, chips)),
        dma((blocks, chips)), dma((blocks, chips)),
        dma((experts,)), dma((experts,)),
        dma((n,)), dma((n,)),
    ]
    cfg = (experts, n, chunk, held * experts * order * width)
    anywhere = pl.BlockSpec(memory_space=pl.ANY)
    back, scale, new_first, new_second = pl.pallas_call(
        functools.partial(kernel, cfg),
        out_shape=(
            jax.ShapeDtypeStruct((order, width), f32),
            jax.ShapeDtypeStruct(tile, f32),
            jax.ShapeDtypeStruct((rows, width), f32),
            jax.ShapeDtypeStruct((rows, width), f32),
        ),
        in_specs=[anywhere] * 5,
        out_specs=(anywhere,) * 4,
        scratch_shapes=scratch,
        compiler_params=pltpu.CompilerParams(
            collective_id=0, has_side_effects=True, vmem_limit_bytes=48 * 1024 * 1024
        ),
    )(
        gradient.reshape(order, width),
        first_moment.reshape(rows, width),
        second_moment.reshape(rows, width),
        left_basis.reshape(order, order),
        right_basis.reshape(blocks, depth, depth),
    )
    return (back / scale[0, 0])[None], new_first[None], new_second[None]


def solution(mesh):
    in_specs = (
        P("expert", "dp", None, None),
        P("expert", "dp", None),
        P("expert", "dp", None),
        P("expert", None, None),
        P("expert", None, None, None),
    )
    out_specs = (P("expert", None, None), P("expert", "dp", None), P("expert", "dp", None))
    return jax.shard_map(
        per_device, mesh=mesh, in_specs=in_specs, out_specs=out_specs, check_vma=False
    )
```

time: 131 us -> 44.1 us (0.34)
  waiting for transfers between devices: 43.4 us -> 0 us
  blocking collectives: 39.1 us -> 0 us
  Pallas kernels: 0 us -> 35.9 us
  matrix products: 22.1 us -> 0 us
  between operations: 14.7 us -> 0.65 us
  local copies, waits for them, and re-layouts: 7.81 us -> 5.03 us
    reduce_scatter x1 -> x0, waiting for transfers between devices: 43.4 us -> none  [per_device(): lax.psum_scatter(jnp.transpose(right_turn(left, right_basis), (1, 0, 2)),...]
    psum x1 -> x0, blocking collectives: 39.1 us -> none  [per_device(): total = lax.psum(jnp.sum(normal * normal), ('expert', 'dp'))]
    pallas_call x0 -> x1, Pallas kernels: none -> 35.9 us  [per_device(): pl.pallas_call(functools.partial(kernel, cfg), out_shape=(jax.ShapeDtypeS...]
    dot_general x4 -> x0, matrix products: 22.1 us -> none  [the longest x1 9.57 us: per_device(): jnp.einsum('ekr,erc->ekc', columns, lax.all_gather(turned, 'dp', axis=1,...]
    another operation x2 -> x0, local copies, waits for them, and re-layouts: 4.18 us -> none  [the longest x1 2.93 us: per_device(): jnp.transpose(right_turn(left, right_basis), (1, 0, 2))]
    reduce_sum x1 -> x0, other arithmetic: 2.5 us -> none  [per_device(): total = lax.psum(jnp.sum(normal * normal), ('expert', 'dp'))]
    broadcast_in_dim x0 -> x1, other arithmetic: none -> 2.27 us  [per_device(): return ((back / scale[0, 0])[None], new_first[None], new_second[None])]
    unnamed x9 -> x8, local copies, waits for them, and re-layouts: 2.9 us -> 4.52 us
  transfers between devices with their start and end apart: 2 -> 0, of which waited for: 1 -> 0; matrix products, arithmetic and copies ran while one was open for 0% -> 0% of each run, Pallas kernels for 0% -> 0%
where the time goes in v1:
time: 44.1 us; the launch traced here: 43.9 us
  Pallas kernels  35.9 us (81%)
  local copies, waits for them, and re-layouts  5.03 us (11%)
  other arithmetic  2.27 us (5%)
  between operations  0.65 us (1%)
    pallas_call x1, Pallas kernels, per_device(): pl.pallas_call(functools.partial(kernel, cfg), out_shape=(jax.ShapeDtypeS...  35.9 us
    unnamed x8, local copies, waits for them, and re-layouts  4.52 us
    broadcast_in_dim x1, other arithmetic, per_device(): return ((back / scale[0, 0])[None], new_first[None], new_second[None])  2.27 us

profile of v1, /device:TPU:1, one launch (start us, length us, event | category | flops | bytes accessed | tf_op | source)
XLA Modules:
  0.0 43.9 jit_solution(15883523752078742593)
XLA Ops:
  0.6 0.0 copy-start
  0.6 1.2 %copy-done = f32[1,512,512]{2,1,0:T(8,128)S(1)} copy-done((f32[1,512,512]{2,1,0:T(8,128)S(1)}, f32[1,512,512]{2,1,0:T(8,128)}, u32[]{:S(2)}) %copy-start) | copy-done | bytes 1048600
  1.9 0.0 copy-start.1
  1.9 0.9 %copy-done.1 = f32[1,64,1024]{2,1,0:T(8,128)S(1)} copy-done((f32[1,64,1024]{2,1,0:T(8,128)S(1)}, f32[1,64,1024]{2,1,0:T(8,128)}, u32[]{:S(2)}) %copy-start.1) | copy-done | bytes 262168
  2.8 0.0 copy-start.2
  2.8 0.9 %copy-done.2 = f32[1,64,1024]{2,1,0:T(8,128)S(1)} copy-done((f32[1,64,1024]{2,1,0:T(8,128)S(1)}, f32[1,64,1024]{2,1,0:T(8,128)}, u32[]{:S(2)}) %copy-start.2) | copy-done | bytes 262168
  3.8 35.9 %shard_map.76 = (f32[512,1024]{1,0:T(8,128)S(1)}, f32[8,128]{1,0:T(8,128)S(1)}, f32[64,1024]{1,0:T(8,128)S(1)}, f32[64,1024]{1,0:T(8,128)S(1)}) custom-call(f32[512,1024]{1,0:T(8,128)} %bitcast.15, f32[64,1024]{1,0:T(8,128)S(1)} %bitcast.11, f32[64,1024]{1,0:T(8,128)S(1)} %bitcast.12, f32[512,512]{1,0:T(8,128)S(1)} %bitcast.10, f32[2,512,512]{2,1,0:T(8,128)} %bitcast.16), custom_call_target="tpu_custom_call" | custom-call | tf_op jit(solution)/shard_map/pallas_call | solution.py:247
  39.7 0.5 %slice.3 = f32[1,1]{1,0:T(1,128)} slice(f32[8,128]{1,0:T(8,128)S(1)} %get-tuple-element.8), slice={[0:1], [0:1]} | slice | bytes 8 | tf_op jit(solution)/shard_map/slice | solution.py:268
  40.2 2.3 %divide_bitcast_fusion = f32[1,512,1024]{2,1,0:T(8,128)} fusion(f32[512,1024]{1,0:T(8,128)S(1)} %get-tuple-element.7, f32[]{:T(128)} %bitcast.5), kind=kLoop, calls=%fused_computation | loop fusion | flops 524288 | bytes 4194308 | tf_op jit(solution)/shard_map/broadcast_in_dim | solution.py:268
  42.5 0.7 %copy.10 = f32[1,64,1024]{2,1,0:T(8,128)} copy(f32[1,64,1024]{2,1,0:T(8,128)S(1)} %bitcast.14) | data formatting | bytes 524288
  43.2 0.7 %copy.11 = f32[1,64,1024]{2,1,0:T(8,128)} copy(f32[1,64,1024]{2,1,0:T(8,128)S(1)} %bitcast.13) | data formatting | bytes 524288
Async XLA Ops:
  0.6 1.2 %copy-start = (f32[1,512,512]{2,1,0:T(8,128)S(1)}, f32[1,512,512]{2,1,0:T(8,128)}, u32[]{:S(2)}) copy-start(f32[1,512,512]{2,1,0:T(8,128)} %param.8) | copy-start | bytes 3145732
  1.9 0.9 %copy-start.1 = (f32[1,64,1024]{2,1,0:T(8,128)S(1)}, f32[1,64,1024]{2,1,0:T(8,128)}, u32[]{:S(2)}) copy-start(f32[1,64,1024]{2,1,0:T(8,128)} %param.6) | copy-start | bytes 786436
  2.8 0.9 %copy-start.2 = (f32[1,64,1024]{2,1,0:T(8,128)S(1)}, f32[1,64,1024]{2,1,0:T(8,128)}, u32[]{:S(2)}) copy-start(f32[1,64,1024]{2,1,0:T(8,128)} %param.7) | copy-start | bytes 786436

commit v2 on v1

--- a/solution.py
+++ b/solution.py
@@ -41,11 +41,11 @@
     chip, core = d // 2, d % 2
     sibling = chip * 2 + (1 - core)
 
-    def other(k):
-        return lax.rem(chip + k, chips) * 2 + core
-
-    def source(k):
-        return lax.rem(chip + chips - k, chips) * 2 + core
+    near = {k: lax.rem(chip + k, chips) for k in range(1, chips)}
+    source = {k: lax.rem(chip + chips - k, chips) for k in range(1, chips)}
+
+    def at(c):
+        return (e, c * 2 + core)
 
     def remote(src, dst, send, recv, to):
         return pltpu.make_async_remote_copy(
@@ -84,7 +84,9 @@
 
     sends = []
     firsts = []
-    for q in range(chunks):
+    seconds = {}
+
+    def for_sibling(q):
         cols = pl.ds(q * chunk, chunk)
         grads[q].wait()
         hi, lo = split(g[:, cols])
@@ -93,38 +95,43 @@
         c = remote(s1.at[q], r1.at[q], s1_s.at[q], s1_r.at[q], (e, sibling))
         c.start()
         firsts.append(c)
-    seconds = {}
-    for q in range(chunks):
+
+    def for_chips(q):
         cols = pl.ds(q * chunk, chunk)
         own = dot3((ah[1], al[1]), (gh[:, cols], gl[:, cols]))
         firsts[q].wait_recv()
         total = own + r1[q]
         for c in range(chips):
-            s2[c, q] = total[c * rows : (c + 1) * rows]
+            s2[q, c] = total[c * rows : (c + 1) * rows]
         for k in range(1, chips):
-            c = remote(
-                s2.at[lax.rem(chip + k, chips), q], r2.at[k, q], s2_s.at[k, q], s2_r.at[k, q], (e, other(k))
-            )
+            c = remote(s2.at[q, near[k]], r2.at[q, k], s2_s.at[q, k], s2_r.at[q, k], at(near[k]))
             c.start()
-            seconds[k, q] = c
+            seconds[q, k] = c
             sends.append(c)
-    lh[...], ll[...] = split(lf[...])
+
+    def summed(q):
+        x = s2[q, chip]
+        for k in range(1, chips):
+            seconds[q, k].wait_recv()
+            x = x + r2[q, k]
+        return x
+
+    for_sibling(0)
+    for q in range(chunks):
+        if q + 1 < chunks:
+            for_sibling(q + 1)
+        for_chips(q)
     for c in loads[1:]:
         c.wait()
     for b in range(blocks):
         rh[b], rl[b] = split(rt[b])
+    lh[...], ll[...] = split(lf[...])
 
     gathers = {}
     forwards = {}
     squares = jnp.zeros((1, 1), jnp.float32)
     for b in range(blocks):
-        parts = []
-        for q in range(b * per, (b + 1) * per):
-            x = s2[chip, q]
-            for k in range(1, chips):
-                seconds[k, q].wait_recv()
-                x = x + r2[k, q]
-            parts.append(x)
+        parts = [summed(q) for q in range(b * per, (b + 1) * per)]
         x = jnp.concatenate(parts, axis=1)
         cols = pl.ds(b * depth, depth)
         turn = (rh[b], rl[b])
@@ -132,15 +139,18 @@
         new_first = 0.9 * fm[:, cols] + 0.1 * mean
         new_second = 0.95 * sm[:, cols] + 0.05 * mean * mean
         normal = new_first / (jnp.sqrt(new_second) + 1e-08)
-        t[b, d] = dot3(split(normal), turn, NT)
-        for k in range(1, chips):
-            c = remote(t.at[b, d], t.at[b, d], ag_s.at[b, k], ag_r.at[b, k], (e, other(k)))
+        turned = dot3(split(normal), turn, NT)
+        for j in range(per):
+            q = b * per + j
+            t[q, d] = turned[:, j * chunk : (j + 1) * chunk]
+            for k in near:
+                c = remote(t.at[q, d], t.at[q, d], ag_s.at[q, k], ag_r.at[q, k], at(near[k]))
+                c.start()
+                gathers[q, k] = c
+                sends.append(c)
+            c = remote(t.at[q, d], t.at[q, d], fw_s.at[q, 0], fw_r.at[q, 0], (e, sibling))
             c.start()
-            gathers[b, k] = c
-            sends.append(c)
-        c = remote(t.at[b, d], t.at[b, d], fw_s.at[b, 0], fw_r.at[b, 0], (e, sibling))
-        c.start()
-        forwards[b, 0] = c
+            forwards[q, 0] = c
         fm[:, cols] = new_first
         sm[:, cols] = new_second
         squares = squares + jnp.sum(
@@ -160,13 +170,15 @@
         c.start()
         tops.append(c)
 
+    def arrive(q, k):
+        gathers[q, k].wait_recv()
+        piece = t.at[q, source[k] * 2 + core]
+        c = remote(piece, piece, fw_s.at[q, k], fw_r.at[q, k], (e, sibling))
+        c.start()
+        forwards[q, k] = c
+
     for b in range(blocks):
-        for k in range(1, chips):
-            gathers[b, k].wait_recv()
-            piece = t.at[b, source(k)]
-            c = remote(piece, piece, fw_s.at[b, k], fw_r.at[b, k], (e, sibling))
-            c.start()
-            forwards[b, k] = c
+        mine = range(b * per, (b + 1) * per)
         if b == 0:
             for c in tops:
                 c.wait_recv()
@@ -176,20 +188,22 @@
                 c = remote(ds.at[d], ds.at[d], d_s.at[k], d_r.at[k], (e, lax.rem(d + k, n)))
                 c.start()
                 peers.append(c)
-        for k in range(chips):
-            forwards[b, k].wait_recv()
-        for j in range(per):
-            cols = pl.ds(b * depth + j * chunk, chunk)
-            piece = t[b, :, :, j * chunk : (j + 1) * chunk].reshape(order, chunk)
-            acc[:, cols] = dot3((lh[...], ll[...]), split(piece))
-        cols = pl.ds(b * depth, depth)
-        c = pltpu.make_async_copy(acc.at[:, cols], back_out.at[:, cols], b_sem.at[b])
-        c.start()
-        outs.append(c)
+        for q in mine:
+            for k in range(1, chips):
+                arrive(q, k)
+        for q in mine:
+            for k in range(chips):
+                forwards[q, k].wait_recv()
+            cols = pl.ds(q * chunk, chunk)
+            acc[:, cols] = dot3((lh[...], ll[...]), split(t[q].reshape(order, chunk)))
+            c = pltpu.make_async_copy(acc.at[:, cols], back_out.at[:, cols], b_sem.at[q])
+            c.start()
+            outs.append(c)
 
     for c in peers:
         c.wait_recv()
-    sc[...] = jnp.sqrt(jnp.sum(ds[...], axis=0) / count + 1e-06)
+    scale = jnp.sqrt(jnp.sum(ds[...], axis=0) / count + 1e-06)
+    sc[...] = jnp.broadcast_to(scale[0:1, 0:1], sc.shape)
     c = pltpu.make_async_copy(sc, scale_out, out_sem.at[2])
     c.start()
     outs.append(c)
@@ -227,18 +241,18 @@
         pltpu.VMEM((blocks, depth, depth), bf16),
         pltpu.VMEM((chunks, half, chunk), f32),
         pltpu.VMEM((chunks, half, chunk), f32),
-        pltpu.VMEM((chips, chunks, rows, chunk), f32),
-        pltpu.VMEM((chips, chunks, rows, chunk), f32),
-        pltpu.VMEM((blocks, n, rows, depth), f32),
+        pltpu.VMEM((chunks, chips, rows, chunk), f32),
+        pltpu.VMEM((chunks, chips, rows, chunk), f32),
+        pltpu.VMEM((chunks, n, rows, chunk), f32),
         pltpu.VMEM((order, width), f32),
         pltpu.VMEM((experts,) + tile, f32),
         pltpu.VMEM((n,) + tile, f32),
-        pltpu.VMEM(tile, f32),
-        dma((4,)), dma((chunks,)), dma((3,)), dma((blocks,)),
+        pltpu.VMEM((1, width), f32),
+        dma((4,)), dma((chunks,)), dma((3,)), dma((chunks,)),
         dma((chunks,)), dma((chunks,)),
-        dma((chips, chunks)), dma((chips, chunks)),
-        dma((blocks, chips)), dma((blocks, chips)),
-        dma((blocks, chips)), dma((blocks, chips)),
+        dma((chunks, chips)), dma((chunks, chips)),
+        dma((chunks, chips)), dma((chunks, chips)),
+        dma((chunks, chips)), dma((chunks, chips)),
         dma((experts,)), dma((experts,)),
         dma((n,)), dma((n,)),
     ]
@@ -248,15 +262,15 @@
         functools.partial(kernel, cfg),
         out_shape=(
             jax.ShapeDtypeStruct((order, width), f32),
-            jax.ShapeDtypeStruct(tile, f32),
+            jax.ShapeDtypeStruct((1, width), f32),
             jax.ShapeDtypeStruct((rows, width), f32),
             jax.ShapeDtypeStruct((rows, width), f32),
         ),
-        in_specs=[anywhere] * 5,
+        in_specs=[pl.BlockSpec(memory_space=pltpu.HBM)] * 5,
         out_specs=(anywhere,) * 4,
         scratch_shapes=scratch,
         compiler_params=pltpu.CompilerParams(
-            collective_id=0, has_side_effects=True, vmem_limit_bytes=48 * 1024 * 1024
+            collective_id=0, has_side_effects=True, vmem_limit_bytes=56 * 1024 * 1024
         ),
     )(
         gradient.reshape(order, width),
@@ -265,7 +279,7 @@
         left_basis.reshape(order, order),
         right_basis.reshape(blocks, depth, depth),
     )
-    return (back / scale[0, 0])[None], new_first[None], new_second[None]
+    return (back / scale)[None], new_first[None], new_second[None]
 
 
 def solution(mesh):

time: 44.1 us -> 41.4 us (0.939)
  local copies, waits for them, and re-layouts: 5.03 us -> 1.41 us
  other arithmetic: 2.27 us -> 3.33 us
    unnamed x8 -> x6, local copies, waits for them, and re-layouts: 4.52 us -> 1.41 us
    broadcast_in_dim x1, other arithmetic: 2.27 us -> 3.33 us  [per_device(): return ((back / scale)[None], new_first[None], new_second[None])]
    slice x1 -> x0, local copies, waits for them, and re-layouts: 0.51 us -> none  [per_device(): return ((back / scale[0, 0])[None], new_first[None], new_second[None])]
where the time goes in v2:
time: 41.4 us; the launch traced here: 41.1 us
  Pallas kernels  35.7 us (86%)
  other arithmetic  3.33 us (8%)
  local copies, waits for them, and re-layouts  1.41 us (3%)
  between operations  0.66 us (2%)
    pallas_call x1, Pallas kernels, per_device(): pl.pallas_call(functools.partial(kernel, cfg), out_shape=(jax.ShapeDtypeS...  35.7 us
    broadcast_in_dim x1, other arithmetic, per_device(): return ((back / scale)[None], new_first[None], new_second[None])  3.33 us
    unnamed x6, local copies, waits for them, and re-layouts  1.41 us

profile of v2, /device:TPU:1, one launch (start us, length us, event | category | flops | bytes accessed | tf_op | source)
XLA Modules:
  0.0 41.1 jit_solution(12732025147811765560)
XLA Ops:
  0.6 35.7 %shard_map.76 = (f32[512,1024]{1,0:T(8,128)}, f32[1,1024]{1,0:T(1,128)}, f32[64,1024]{1,0:T(8,128)}, f32[64,1024]{1,0:T(8,128)}) custom-call(f32[512,1024]{1,0:T(8,128)} %bitcast.10, f32[64,1024]{1,0:T(8,128)} %bitcast.13, f32[64,1024]{1,0:T(8,128)} %bitcast.14, f32[512,512]{1,0:T(8,128)} %bitcast.12, f32[2,512,512]{2,1,0:T(8,128)} %bitcast.11), custom_call_target="tpu_custom_call" | custom-call | tf_op jit(solution)/shard_map/pallas_call | solution.py:261
  36.3 0.0 copy-start.1
  36.3 0.0 copy-start
  36.3 3.3 %divide_bitcast_fusion = f32[1,512,1024]{2,1,0:T(8,128)} fusion(f32[512,1024]{1,0:T(8,128)} %get-tuple-element.7, f32[1024]{0:T(1024)} %bitcast.17), kind=kLoop, calls=%fused_computation | loop fusion | flops 524288 | bytes 4198400 | tf_op jit(solution)/shard_map/broadcast_in_dim | solution.py:282
  39.7 0.0 copy-done.1
  39.7 0.7 %copy.10 = f32[1,64,1024]{2,1,0:T(8,128)} copy(f32[1,64,1024]{2,1,0:T(8,128)S(1)} %bitcast.16) | data formatting | bytes 524288
  40.4 0.0 copy-done
  40.4 0.7 %copy.11 = f32[1,64,1024]{2,1,0:T(8,128)} copy(f32[1,64,1024]{2,1,0:T(8,128)S(1)} %bitcast.15) | data formatting | bytes 524288
Async XLA Ops:
  36.3 3.4 %copy-start.1 = (f32[64,1024]{1,0:T(8,128)S(1)}, f32[64,1024]{1,0:T(8,128)}, u32[]{:S(2)}) copy-start(f32[64,1024]{1,0:T(8,128)} %get-tuple-element.9) | copy-start | bytes 786436
  36.3 4.0 %copy-start = (f32[64,1024]{1,0:T(8,128)S(1)}, f32[64,1024]{1,0:T(8,128)}, u32[]{:S(2)}) copy-start(f32[64,1024]{1,0:T(8,128)} %get-tuple-element.10) | copy-start | bytes 786436
